TPU v7x, 256 devices: a whole 4x4x8 slice. The times are simulated.
256 devices in a mesh: col: 128 (over x, y, z), layer: 2 (over core).
Axes of the slice: x: 4, y: 4, z: 8, core: 2. Of those that a mesh axis runs over, the one named last changes fastest.
Arguments:
- screens: float32 [2, 8192, 8192], P('layer', 'col'), may hold values from -12 to 12
- strips: float32 [2, 32, 8192], P('layer'), may hold values from -12 to 12
- wind_cols: int32 [2], replicated, may hold values from 1 to 32, as said below
- wind_rows: int32 [2], replicated, may hold values from -1024 to 1024
- heights: int32 [2], replicated, may hold values from 64 to 256
Outputs:
- pupil_field: float32 [2, 8192, 8192], P(None, ('col', 'layer'))
- next_screens: float32 [2, 8192, 8192], P('layer', 'col')
Inputs may be any that keep to these rules, and one draw needn't show every extreme that they name: `wind_cols`: the layers move by distinct numbers of columns, and some layer moves by exactly 32.
All inputs are finite; a program needn't handle non-finite values.
Results may differ from a plain program's by a relative error of at most 0.00022.
Values sent between devices are 32-bit elements; how exact they have to be, the bound alone decides.
A program may use at most 128 MiB of HBM per device.

v0:
```python
import math

import jax
import jax.numpy as jnp
from jax import lax
from jax.sharding import PartitionSpec as P


def passed_along(value, axis, steps):
    count = lax.axis_size(axis)
    leading, last = (max(0, -steps), min(count, count - steps))
    return lax.ppermute(value, axis, [(source, source + steps) for source in range(leading, last)])


def fresnel_angle(frequency, distance, size):
    signed = jnp.where(frequency < size // 2, frequency, frequency - size)
    square = signed * signed
    high = square // size
    low = square % size
    count = (distance * high % size * size + distance * low) % (size * size)
    return 2.0 * math.pi / (size * size) * count.astype(jnp.float32)


def unit_table(rows, columns, modulus):
    left = lax.broadcasted_iota(jnp.int32, (rows, columns), 0)
    right = lax.broadcasted_iota(jnp.int32, (rows, columns), 1)
    angle = 2.0 * math.pi / modulus * (left * right % modulus).astype(jnp.float32)
    return (jnp.cos(angle), -jnp.sin(angle))


def complex_table(real_part, imag_part):
    return jnp.stack([jnp.stack([real_part, imag_part], 1), jnp.stack([-imag_part, real_part], 1)])


def complex_sum(form, field, table):
    return jnp.einsum(form, field, table, precision=lax.Precision.HIGHEST)


def twist(field, cosine, sine):
    real = field[0]
    imaginary = field[1]
    return jnp.stack([real * cosine - imaginary * sine, real * sine + imaginary * cosine])


def forward_last(field, tables):
    fwd_first, fwd_second, inv_first, inv_second, twiddle = tables
    parts, rows, size = field.shape
    shaped = field.reshape(parts, rows, fwd_first.shape[1], fwd_second.shape[1])
    shaped = complex_sum("crmn,cmdk->drkn", shaped, fwd_first)
    shaped = twist(shaped, twiddle[0], twiddle[1])
    shaped = complex_sum("crkn,cndj->drkj", shaped, fwd_second)
    return shaped.reshape(parts, rows, size)


def inverse_last(field, tables):
    fwd_first, fwd_second, inv_first, inv_second, twiddle = tables
    parts, rows, size = field.shape
    shaped = field.reshape(parts, rows, inv_first.shape[1], inv_second.shape[1])
    shaped = complex_sum("crkj,cjdn->drkn", shaped, inv_second)
    shaped = twist(shaped, twiddle[0], -twiddle[1])
    shaped = complex_sum("crkn,ckdm->drmn", shaped, inv_first)
    return shaped.reshape(parts, rows, size) / size


def forward_first(field, tables):
    fwd_first, fwd_second, inv_first, inv_second, twiddle = tables
    parts, size, width = field.shape
    shaped = field.reshape(parts, fwd_first.shape[1], fwd_second.shape[1], width)
    shaped = complex_sum("cmnb,cmdk->dbkn", shaped, fwd_first)
    shaped = twist(shaped, twiddle[0], twiddle[1])
    return complex_sum("cbkn,cndj->dbkj", shaped, fwd_second)


def inverse_first(field, tables):
    fwd_first, fwd_second, inv_first, inv_second, twiddle = tables
    parts, width = (field.shape[0], field.shape[1])
    size = inv_first.shape[1] * inv_second.shape[1]
    shaped = complex_sum("cbkj,cjdn->dbkn", field, inv_second)
    shaped = twist(shaped, twiddle[0], -twiddle[1])
    shaped = complex_sum("cbkn,ckdm->dmnb", shaped, inv_first)
    return shaped.reshape(parts, size, width) / size


def rotate(field, phase):
    return twist(field, jnp.cos(phase), jnp.sin(phase))


def propagate(field, distance, tables, regroup, ungroup, offset):
    first_len = tables[0].shape[1]
    second_len = tables[1].shape[1]
    size = field.shape[2]
    field = forward_last(field, tables)
    field = regroup(field)
    field = lax.all_to_all(field, "col", split_axis=2, concat_axis=1, tiled=True)
    width = field.shape[2]
    slot = offset + lax.axis_index("col") * width + lax.iota(jnp.int32, width)
    freq_rows = slot // second_len + first_len * (slot % second_len)
    angle_rows = fresnel_angle(freq_rows, distance, size)
    lower = lax.broadcasted_iota(jnp.int32, (first_len, second_len), 0)
    upper = lax.broadcasted_iota(jnp.int32, (first_len, second_len), 1)
    angle_cols = fresnel_angle(lower + first_len * upper, distance, size)
    angle = angle_rows[:, None, None] + angle_cols[None, :, :]
    spectrum = forward_first(field, tables)
    spectrum = twist(spectrum, jnp.cos(angle), -jnp.sin(angle))
    field = inverse_first(spectrum, tables)
    field = lax.all_to_all(field, "col", split_axis=1, concat_axis=2, tiled=True)
    field = ungroup(field)
    return inverse_last(field, tables)


def on_device(screens, strips, wind_cols, wind_rows, heights):
    layers_here, span, size = screens.shape
    reach = strips.shape[1]
    group = lax.axis_index("layer")
    groups = lax.axis_size("layer")
    edge = screens[:, span - reach :, :]
    came = passed_along(edge, "col", 1)
    came = jnp.where(lax.axis_index("col") == 0, strips, came)
    extended = jnp.concatenate([came, screens], axis=1)
    layer = group * layers_here + 0
    start = reach - wind_cols[layer]
    window = lax.dynamic_slice_in_dim(extended[0], start, span, 0)
    moved = [jnp.roll(window, wind_rows[layer], axis=1)]
    next_screens = jnp.stack(moved)
    first_len = size // 128
    first_table = unit_table(first_len, first_len, first_len)
    second_table = unit_table(128, 128, 128)
    tables = (
        complex_table(first_table[0], first_table[1]),
        complex_table(second_table[0], second_table[1]),
        complex_table(first_table[0], -first_table[1]),
        complex_table(second_table[0], -second_table[1]),
        unit_table(first_len, 128, size),
    )
    share = lax.all_to_all(next_screens, "layer", split_axis=1, concat_axis=0, tiled=True)

    def regroup(field):
        return lax.all_to_all(field, "layer", split_axis=2, concat_axis=1, tiled=True)

    def ungroup(field):
        return lax.all_to_all(field, "layer", split_axis=1, concat_axis=2, tiled=True)

    offset = group * (size // groups)
    field = jnp.stack([jnp.cos(share[0]), jnp.sin(share[0])])
    for layer in range(share.shape[0]):
        if layer > 0:
            field = rotate(field, share[layer])
        field = propagate(field, heights[layer], tables, regroup, ungroup, offset)
    return (field, next_screens)


def solution(mesh):
    placed = (P("layer", "col", None), P("layer", None, None), P(), P(), P())
    return jax.shard_map(
        on_device,
        mesh=mesh,
        in_specs=placed,
        out_specs=(P(None, ("col", "layer"), None), P("layer", "col", None)),
        check_vma=False,
    )
```

profile of v0, /device:TPU:1, one launch (start us, length us, event | category | flops | bytes accessed | tf_op | source)
XLA Modules:
  0.0 652.6 jit_solution(406460399348113755)
XLA Ops:
  13.1 16.4 %collective-permute-done = f32[1,32,8192]{2,1,0:T(8,128)S(1)} collective-permute-done((f32[1,32,8192]{2,1,0:T(8,128)}, f32[1,32,8192]{2,1,0:T(8,128)S(1)}, u32[]{:S(2)}, u32[]{:S(2)}) %collective-permute-start) | collective-permute-done | bytes 1048608 | tf_op jit(solution)/shard_map/ppermute | solution.py:12
  33.3 7.0 %all_to_all.144 = f32[1,64,8192]{2,0,1:T(1,128)S(1)} all-to-all(f32[1,64,8192]{2,0,1:T(1,128)S(1)} %copy.199), channel_id=1, replica_groups=mesh['col'=128,'layer'=2] {'layer'}, dimensions={1} | all-to-all | bytes 4194304 | tf_op jit(solution)/shard_map/all_to_all | solution.py:135
  54.8 20.7 %reshape.568 = f32[2,1,262144]{2,1,0:T(1,128)S(1)} reshape(f32[8192,2,32]{2,1,0:T(2,128)} %bitcast.322) | data formatting | bytes 4194304
  75.5 6.3 all_to_all.145
  82.4 8.1 %reduce = f32[2,262144]{1,0:T(2,128)S(1)} reduce(f32[2,1,262144]{2,1,0:T(1,128)} %all_to_all.145, f32[]{:T(128)} %broadcast.1149), dimensions={1}, to_apply=%all_to_all.107.reduce_sub_computation | reduce | bytes 4194308 | tf_op jit(solution)/shard_map/all_to_all | solution.py:138
  90.5 11.2 %reshape.569 = f32[8192,2,32]{2,1,0:T(2,128)} reshape(f32[2,262144]{1,0:T(2,128)S(1)} %reduce) | data formatting | bytes 4194304
  101.7 9.7 %copy.204 = f32[2,2,32,4096]{3,2,1,0:T(8,128)S(1)} copy(f32[2,2,32,4096]{2,0,3,1:T(2,128)} %bitcast.323) | data formatting | bytes 4194304 | tf_op jit(solution)/shard_map/all_to_all | solution.py:138
  115.8 6.9 %reshape.570 = f32[128,1,4096]{2,1,0:T(1,128)} reshape(f32[4096,2,64]{2,1,0:T(2,128)} %bitcast.332) | data formatting | bytes 4194304
  122.7 17.8 %all-to-all-start.2 = ((f32[128,1,4096]{2,1,0:T(1,128)}), f32[128,1,4096]{2,1,0:T(1,128)}, u32[]{:S(2)}, u32[]{:S(2)}) async-start(f32[128,1,4096]{2,1,0:T(1,128)} %reshape.570), calls=%async_computation.2 | async-start | bytes 4194304 | tf_op jit(solution)/shard_map/all_to_all | solution.py:94
  144.5 48.5 %all-to-all-done.2 = f32[128,1,4096]{2,1,0:T(1,128)} async-done(((f32[128,1,4096]{2,1,0:T(1,128)}), f32[128,1,4096]{2,1,0:T(1,128)}, u32[]{:S(2)}, u32[]{:S(2)}) %all-to-all-start.2) | async-done | bytes 2097184 | tf_op jit(solution)/shard_map/all_to_all | solution.py:94
  193.0 7.3 %reduce.1 = f32[128,4096]{1,0:T(8,128)S(1)} reduce(f32[128,1,4096]{2,1,0:T(1,128)} %all-to-all-done.2, f32[]{:T(128)} %broadcast.1149), dimensions={1}, to_apply=%all_to_all.111.reduce_sub_computation | reduce | bytes 4194308 | tf_op jit(solution)/shard_map/all_to_all | solution.py:94
  234.0 10.8 %reshape.572 = f32[128,1,4096]{2,1,0:T(1,128)} reshape(f32[8192,2,32]{2,1,0:T(2,128)} %bitcast.324) | data formatting | bytes 4194304
  244.8 7.7 %all-to-all-start.3 = ((f32[128,1,4096]{2,1,0:T(1,128)}), f32[128,1,4096]{2,1,0:T(1,128)}, u32[]{:S(2)}, u32[]{:S(2)}) async-start(f32[128,1,4096]{2,1,0:T(1,128)} %reshape.572), calls=%async_computation.3 | async-start | bytes 4194304 | tf_op jit(solution)/shard_map/all_to_all | solution.py:106
  252.6 50.6 %all-to-all-done.3 = f32[128,1,4096]{2,1,0:T(1,128)} async-done(((f32[128,1,4096]{2,1,0:T(1,128)}), f32[128,1,4096]{2,1,0:T(1,128)}, u32[]{:S(2)}, u32[]{:S(2)}) %all-to-all-start.3) | async-done | bytes 2097184 | tf_op jit(solution)/shard_map/all_to_all | solution.py:106
  303.2 7.3 %reduce.2 = f32[128,4096]{1,0:T(8,128)S(1)} reduce(f32[128,1,4096]{2,1,0:T(1,128)} %all-to-all-done.3, f32[]{:T(128)} %broadcast.1149), dimensions={1}, to_apply=%all_to_all.114.reduce_sub_computation | reduce | bytes 4194308 | tf_op jit(solution)/shard_map/all_to_all | solution.py:106
  310.5 8.5 %reshape.573 = f32[8192,2,32]{2,1,0:T(2,128)} reshape(f32[128,4096]{1,0:T(8,128)S(1)} %reduce.2) | data formatting | bytes 4194304
  319.0 10.9 %copy.296 = f32[2,128,64,32]{2,3,1,0:T(8,128)} copy(f32[2,128,64,32]{3,0,2,1:T(2,128)} %bitcast.325) | data formatting | bytes 4194304 | tf_op jit(solution)/shard_map/all_to_all | solution.py:106
  333.8 9.6 %all_to_all.146 = f32[2,64,4096]{2,0,1:T(2,128)S(1)} all-to-all(f32[2,64,4096]{2,0,1:T(2,128)S(1)} %copy.217), channel_id=1, replica_groups=mesh['col'=128,'layer'=2] {'layer'}, dimensions={1} | all-to-all | bytes 4194304 | tf_op jit(solution)/shard_map/all_to_all | solution.py:141
  374.5 10.2 %reshape.574 = f32[2,1,262144]{2,1,0:T(1,128)S(1)} reshape(f32[8192,2,32]{2,1,0:T(2,128)} %bitcast.326) | data formatting | bytes 4194304
  384.7 6.5 all_to_all.147
  391.2 8.1 %reduce.3 = f32[2,262144]{1,0:T(2,128)S(1)} reduce(f32[2,1,262144]{2,1,0:T(1,128)} %all_to_all.147, f32[]{:T(128)} %broadcast.1149), dimensions={1}, to_apply=%all_to_all.121.reduce_sub_computation | reduce | bytes 4194308 | tf_op jit(solution)/shard_map/all_to_all | solution.py:138
  399.3 11.2 %reshape.575 = f32[8192,2,32]{2,1,0:T(2,128)} reshape(f32[2,262144]{1,0:T(2,128)S(1)} %reduce.3) | data formatting | bytes 4194304
  410.5 9.7 %copy.229 = f32[2,2,32,4096]{3,2,1,0:T(8,128)S(1)} copy(f32[2,2,32,4096]{2,0,3,1:T(2,128)} %bitcast.327) | data formatting | bytes 4194304 | tf_op jit(solution)/shard_map/all_to_all | solution.py:138
  424.7 6.1 reshape.576
  430.8 59.3 %all_to_all.148 = f32[128,1,4096]{2,1,0:T(1,128)} all-to-all(f32[128,1,4096]{2,1,0:T(1,128)S(1)} %reshape.576), channel_id=1, replica_groups=mesh['col'=128,'layer'=2] {'col'}, dimensions={0} | all-to-all | bytes 4194304 | tf_op jit(solution)/shard_map/all_to_all | solution.py:94
  490.1 7.3 %reduce.4 = f32[128,4096]{1,0:T(8,128)S(1)} reduce(f32[128,1,4096]{2,1,0:T(1,128)} %all_to_all.148, f32[]{:T(128)} %broadcast.1149), dimensions={1}, to_apply=%all_to_all.125.reduce_sub_computation | reduce | bytes 4194308 | tf_op jit(solution)/shard_map/all_to_all | solution.py:94
  531.5 10.1 %reshape.578 = f32[128,1,4096]{2,1,0:T(1,128)S(1)} reshape(f32[8192,2,32]{2,1,0:T(2,128)} %bitcast.328) | data formatting | bytes 4194304
  541.6 57.7 %all_to_all.149 = f32[128,1,4096]{2,1,0:T(1,128)} all-to-all(f32[128,1,4096]{2,1,0:T(1,128)S(1)} %reshape.578), channel_id=1, replica_groups=mesh['col'=128,'layer'=2] {'col'}, dimensions={0} | all-to-all | bytes 4194304 | tf_op jit(solution)/shard_map/all_to_all | solution.py:106
  599.3 7.3 %reduce.5 = f32[128,4096]{1,0:T(8,128)S(1)} reduce(f32[128,1,4096]{2,1,0:T(1,128)} %all_to_all.149, f32[]{:T(128)} %broadcast.1149), dimensions={1}, to_apply=%all_to_all.128.reduce_sub_computation | reduce | bytes 4194308 | tf_op jit(solution)/shard_map/all_to_all | solution.py:106
  606.6 8.5 %reshape.579 = f32[8192,2,32]{2,1,0:T(2,128)} reshape(f32[128,4096]{1,0:T(8,128)S(1)} %reduce.5) | data formatting | bytes 4194304
  615.1 10.9 %copy.303 = f32[2,128,64,32]{2,3,1,0:T(8,128)} copy(f32[2,128,64,32]{3,0,2,1:T(2,128)} %bitcast.329) | data formatting | bytes 4194304 | tf_op jit(solution)/shard_map/all_to_all | solution.py:106
  629.9 9.4 %all_to_all.150 = f32[2,64,4096]{2,0,1:T(2,128)S(1)} all-to-all(f32[2,64,4096]{2,0,1:T(2,128)S(1)} %copy.242), channel_id=1, replica_groups=mesh['col'=128,'layer'=2] {'layer'}, dimensions={1} | all-to-all | bytes 4194304 | tf_op jit(solution)/shard_map/all_to_all | solution.py:141
  (141 shorter events, 159.8 us)
Async XLA Ops:
  0.6 6.8 %copy-start.27 = (s32[2]{0:T(128)S(1)}, s32[2]{0:T(128)}, u32[]{:S(2)}) copy-start(s32[2]{0:T(128)} %param.8) | copy-start | bytes 28
  0.6 9.4 %copy-start.28 = (s32[2]{0:T(128)S(1)}, s32[2]{0:T(128)}, u32[]{:S(2)}) copy-start(s32[2]{0:T(128)} %param.7) | copy-start | bytes 28
  0.7 28.9 %copy-start.19 = (f32[1,32,8192]{2,1,0:T(8,128)S(1)}, f32[1,32,8192]{2,1,0:T(8,128)}, u32[]{:S(2)}) copy-start(f32[1,32,8192]{2,1,0:T(8,128)} %param.6) | copy-start | bytes 3145732
  3.0 26.5 %collective-permute-start = (f32[1,32,8192]{2,1,0:T(8,128)}, f32[1,32,8192]{2,1,0:T(8,128)S(1)}, u32[]{:S(2)}, u32[]{:S(2)}) collective-permute-start(f32[1,32,8192]{2,1,0:T(8,128)} %slice.90), channel_id=1, source_target_pairs={{0,2},{2,4},{4,6},{6,8},{8,10},{10,12},{12,14},{14,16},{16,18},{18... | collective-permute-start | bytes 3145736 | tf_op jit(solution)/shard_map/ppermute | solution.py:12
  12.6 204.4 %copy-start.20 = (f32[64,128]{1,0:T(8,128)}, f32[64,128]{1,0:T(8,128)S(1)}, u32[]{:S(2)}) copy-start(f32[64,128]{1,0:T(8,128)S(1)} %get-tuple-element.51) | copy-start | bytes 98308
  12.6 212.9 %copy-start.6 = (f32[64,128]{1,0:T(8,128)}, f32[64,128]{1,0:T(8,128)S(1)}, u32[]{:S(2)}) copy-start(f32[64,128]{1,0:T(8,128)S(1)} %get-tuple-element.50) | copy-start | bytes 98308
  12.9 16.7 %copy-start.3 = (f32[1,64,8192]{2,1,0:T(8,128)S(1)}, f32[1,64,8192]{2,1,0:T(8,128)}, u32[]{:S(2)}) copy-start(f32[1,64,8192]{2,1,0:T(8,128)} %param.5) | copy-start | bytes 6291460
  13.0 202.0 %copy-start.15 = (f32[1,64,2,64]{1,3,0,2:T(8,128)}, f32[1,64,2,64]{1,3,0,2:T(8,128)S(1)}, u32[]{:S(2)}) copy-start(f32[1,64,2,64]{1,3,0,2:T(8,128)S(1)} %get-tuple-element.35) | copy-start | bytes 98308
  13.0 202.0 %copy-start.17 = (f32[1,64,2,64]{1,3,0,2:T(8,128)}, f32[1,64,2,64]{1,3,0,2:T(8,128)S(1)}, u32[]{:S(2)}) copy-start(f32[1,64,2,64]{1,3,0,2:T(8,128)S(1)} %get-tuple-element.40) | copy-start | bytes 98308
  13.0 213.0 %copy-start.9 = (f32[1,64,2,64]{1,3,2,0:T(8,128)}, f32[1,64,2,64]{1,3,2,0:T(8,128)S(1)}, u32[]{:S(2)}) copy-start(f32[1,64,2,64]{1,3,2,0:T(8,128)S(1)} %get-tuple-element.34) | copy-start | bytes 98308
  13.0 213.0 %copy-start.12 = (f32[1,64,2,64]{1,3,2,0:T(8,128)}, f32[1,64,2,64]{1,3,2,0:T(8,128)S(1)}, u32[]{:S(2)}) copy-start(f32[1,64,2,64]{1,3,2,0:T(8,128)S(1)} %get-tuple-element.41) | copy-start | bytes 98308
  13.1 204.4 %copy-start.4 = (f32[1,128,2,128]{3,1,0,2:T(8,128)}, f32[1,128,2,128]{3,1,0,2:T(8,128)S(1)}, u32[]{:S(2)}) copy-start(f32[1,128,2,128]{3,1,0,2:T(8,128)S(1)} %get-tuple-element.38) | copy-start | bytes 393220
  31.1 9.1 %copy-start = (f32[1,64,8192]{2,1,0:T(8,128)}, f32[1,64,8192]{2,1,0:T(8,128)S(1)}, u32[]{:S(2)}) copy-start(f32[1,64,8192]{2,1,0:T(8,128)S(1)} %fusion.3) | copy-start | bytes 6291460
  40.3 3.9 copy-start.1
  122.7 17.9 %copy-start.26 = (s32[2]{0:T(128)S(1)}, s32[2]{0:T(128)}, u32[]{:S(2)}) copy-start(s32[2]{0:T(128)} %param.9) | copy-start | bytes 28
  122.7 70.3 %all-to-all-start.2 = ((f32[128,1,4096]{2,1,0:T(1,128)}), f32[128,1,4096]{2,1,0:T(1,128)}, u32[]{:S(2)}, u32[]{:S(2)}) async-start(f32[128,1,4096]{2,1,0:T(1,128)} %reshape.570), calls=%async_computation.2 | async-start | bytes 4194304 | tf_op jit(solution)/shard_map/all_to_all | solution.py:94
  142.5 83.0 %copy-start.22 = (f32[64,128]{1,0:T(8,128)}, f32[64,128]{1,0:T(8,128)S(1)}, u32[]{:S(2)}) copy-start(f32[64,128]{1,0:T(8,128)S(1)} %fusion.139) | copy-start | bytes 98308
  244.8 7.7 %copy-start.2 = (f32[1,64,8192]{2,0,1:T(1,128)S(1)}, f32[1,64,8192]{2,0,1:T(1,128)}, u32[]{:S(2)}) copy-start(f32[1,64,8192]{2,0,1:T(1,128)} %copy-done.1) | copy-start | bytes 6291460
  244.8 58.4 %all-to-all-start.3 = ((f32[128,1,4096]{2,1,0:T(1,128)}), f32[128,1,4096]{2,1,0:T(1,128)}, u32[]{:S(2)}, u32[]{:S(2)}) async-start(f32[128,1,4096]{2,1,0:T(1,128)} %reshape.572), calls=%async_computation.3 | async-start | bytes 4194304 | tf_op jit(solution)/shard_map/all_to_all | solution.py:106
  349.1 3.5 copy-start.7
  349.1 3.5 copy-start.23
  352.6 0.8 copy-start.10
  352.6 0.9 copy-start.13
  362.9 0.8 copy-start.16
  362.9 0.9 copy-start.18
  363.8 2.0 copy-start.8
  363.8 2.0 copy-start.21
  365.8 0.9 copy-start.5
  514.5 1.9 copy-start.25
  520.7 1.9 copy-start.24
  522.7 0.8 copy-start.11
  522.7 0.9 copy-start.14
where the time goes:
time: 659 us; the launch traced here: 653 us
  local copies, waits for them, and re-layouts  246 us (37%)
  blocking collectives  156 us (24%)
  waiting for transfers between devices  116 us (18%)
  other arithmetic  67.5 us (10%)
  matrix products  32.5 us (5%)
  starting transfers between devices  29.9 us (5%)
    unnamed x75, local copies, waits for them, and re-layouts  120 us
    all_to_all x1, blocking collectives, propagate(): lax.all_to_all(field, 'col', split_axis=2, concat_axis=1, tiled=True)  59.3 us
    all_to_all x1, blocking collectives, propagate(): lax.all_to_all(field, 'col', split_axis=1, concat_axis=2, tiled=True)  57.7 us
    all_to_all x1, waiting for transfers between devices, propagate(): lax.all_to_all(field, 'col', split_axis=1, concat_axis=2, tiled=True)  50.6 us
    all_to_all x1, waiting for transfers between devices, propagate(): lax.all_to_all(field, 'col', split_axis=2, concat_axis=1, tiled=True)  48.5 us
    dot_general x16, matrix products, complex_sum(): return jnp.einsum(form, field, table, precision=lax.Precision.HIGHEST)  32.5 us
    all_to_all x4, local copies, waits for them, and re-layouts, propagate(): lax.all_to_all(field, 'col', split_axis=1, concat_axis=2, tiled=True)  29.5 us
    all_to_all x5, local copies, waits for them, and re-layouts, regroup(): lax.all_to_all(field, 'layer', split_axis=2, concat_axis=1, tiled=True)  28.9 us
  transfers between devices with their start and end apart: 3, of which 3 were waited for; matrix products, arithmetic and copies ran while one was open for 1% of the time, Pallas kernels for 0%

commit v1 on v0

v1 whole, which is shorter than its diff:
```python
import functools
import math

import jax
import jax.numpy as jnp
import numpy as np
from jax import lax
from jax.experimental import pallas as pl
from jax.experimental.pallas import tpu as pltpu
from jax.sharding import PartitionSpec as P

MESH = pl.DeviceIdType.MESH
F32 = jnp.float32
BF16 = jnp.bfloat16

SIZE = 8192
LANES = 128
SPAN = 64
REACH = 32
CHIPS = 128
DEVICES = 256
STEPS = 8


def cut(table):
    high = table.astype(np.float32).astype(BF16)
    low = (table - high.astype(np.float64)).astype(np.float32).astype(BF16)
    return high, low


def dft(count, sign):
    index = np.arange(count)
    return np.exp(sign * 2j * np.pi * (np.outer(index, index) % count) / count)


def left_complex(table):
    return np.block([[table.real, -table.imag], [table.imag, table.real]])


def right_complex(table):
    return np.block([[table.real, table.imag], [-table.imag, table.real]])


def left_half(table):
    high, low = cut(left_complex(table))
    return np.block([[high, high], [low, np.zeros_like(low)]])


def left_full(table):
    high, low = cut(left_complex(table))
    return np.concatenate([high, low, high], 1)


def right_full(table):
    high, low = cut(right_complex(table))
    return np.concatenate([high, low, high], 0)


def tables_y():
    twiddle = np.exp(-2j * np.pi * np.outer(np.arange(64), np.arange(128)) / SIZE)
    return [
        left_half(dft(64, -1)),
        left_half(dft(64, 1)),
        right_full(dft(128, -1)),
        right_full(dft(128, 1)),
        np.stack([twiddle.real, twiddle.imag]).astype(np.float32),
    ]


def tables_x():
    twiddle = np.exp(-2j * np.pi * np.outer(np.arange(128), np.arange(64)) / SIZE)
    twiddle = np.concatenate([twiddle, twiddle], 1)
    pair = np.eye(2)
    return [
        left_full(dft(128, -1)),
        left_full(dft(128, 1)),
        right_full(np.kron(pair, dft(64, -1))),
        right_full(np.kron(pair, dft(64, 1))),
        np.stack([twiddle.real, twiddle.imag]).astype(np.float32),
    ]


def wave(angle):
    square = angle * angle
    sine = -1.9515295891e-4 * square + 8.3321608736e-3
    sine = sine * square - 1.6666654611e-1
    sine = sine * square * angle + angle
    cosine = 2.443315711809948e-5 * square - 1.388731625493765e-3
    cosine = cosine * square + 4.166664568298827e-2
    cosine = cosine * square * square - 0.5 * square + 1.0
    return cosine, sine


def turned(cosine, sine, quarter):
    odd = (quarter & 1) == 1
    first = jnp.where(odd, sine, cosine)
    second = jnp.where(odd, cosine, sine)
    first = jnp.where(((quarter + 1) & 2) == 2, -first, first)
    second = jnp.where((quarter & 2) == 2, -second, second)
    return first, second


def cos_sin(angle):
    count = jnp.floor(angle * (2.0 / math.pi) + 0.5)
    rest = angle - count * 1.5703125
    rest = rest - count * 4.837512969970703125e-4
    rest = rest - count * 7.54978995489188216e-8
    cosine, sine = wave(rest)
    return turned(cosine, sine, count.astype(jnp.int32))


def symbol(frequency, distance, shift):
    signed = jnp.where(frequency < SIZE // 2, frequency, frequency - SIZE)
    count = (distance * signed * signed + shift * signed * SIZE) & (SIZE * SIZE - 1)
    unit = SIZE * SIZE // 4
    quarter = (count + unit // 2) // unit
    rest = (count - quarter * unit).astype(F32) * (2.0 * math.pi / (SIZE * SIZE))
    cosine, sine = wave(rest)
    cosine, sine = turned(cosine, sine, quarter)
    return cosine * (1.0 / SIZE), sine * (-1.0 / SIZE)


def split(value):
    high = value.astype(BF16)
    low = (value - high.astype(F32)).astype(BF16)
    return high, low


def dot(left, right):
    return jnp.dot(left, right, preferred_element_type=F32)


def apply_left_half(table, value):
    high, low = split(value)
    both = dot(table, jnp.concatenate([high, low], 0))
    rows = both.shape[0] // 2
    return both[:rows] + both[rows:]


def apply_left(table, value):
    high, low = split(value)
    return dot(table, jnp.concatenate([high, high, low], 0))


def apply_right(value, table):
    high, low = split(value)
    return dot(jnp.concatenate([high, high, low], 1), table)


def times(real, imag, other_real, other_imag):
    return (
        real * other_real - imag * other_imag,
        real * other_imag + imag * other_real,
    )


def symbol_y(ref, distance, shift):
    rows = lax.broadcasted_iota(jnp.int32, (64, 128), 0)
    lanes = lax.broadcasted_iota(jnp.int32, (64, 128), 1)
    ref[0], ref[1] = symbol(rows + 64 * lanes, distance, shift)


def symbol_x(ref, distance, shift):
    rows = lax.broadcasted_iota(jnp.int32, (128, 128), 0)
    lanes = lax.broadcasted_iota(jnp.int32, (128, 128), 1)
    ref[0], ref[1] = symbol(rows + 128 * (lanes % 64), distance, shift)


def along_y(src, dst, width, tables, phase):
    fwd_left, inv_left, fwd_right, inv_right, twiddle = tables
    together = 4

    def body(group, carry):
        first = group * together
        fields = []
        for i in range(together):
            rows = pl.ds(first + i, 64, stride=width)
            fields.append(jnp.concatenate([src[0, rows, :], src[1, rows, :]], 0))
        value = apply_left_half(fwd_left[...], jnp.concatenate(fields, 1))
        tw_real, tw_imag = twiddle[0], twiddle[1]
        pieces = []
        for i in range(together):
            lanes = slice(i * 128, (i + 1) * 128)
            pieces.append(
                jnp.concatenate(
                    times(value[:64, lanes], value[64:, lanes], tw_real, tw_imag), 1
                )
            )
        value = apply_right(jnp.concatenate(pieces, 0), fwd_right[...])
        ph_real, ph_imag = phase[0], phase[1]
        pieces = []
        for i in range(together):
            rows = slice(i * 64, (i + 1) * 64)
            pieces.append(
                jnp.concatenate(
                    times(value[rows, :128], value[rows, 128:], ph_real, ph_imag), 1
                )
            )
        value = apply_right(jnp.concatenate(pieces, 0), inv_right[...])
        fields = []
        for i in range(together):
            rows = slice(i * 64, (i + 1) * 64)
            fields.append(
                jnp.concatenate(
                    times(value[rows, :128], value[rows, 128:], tw_real, -tw_imag), 0
                )
            )
        value = apply_left_half(inv_left[...], jnp.concatenate(fields, 1))
        for i in range(together):
            rows = pl.ds(first + i, 64, stride=width)
            lanes = slice(i * 128, (i + 1) * 128)
            dst[0, rows, :] = value[:64, lanes]
            dst[1, rows, :] = value[64:, lanes]
        return carry

    lax.fori_loop(0, width // together, body, 0)


def along_x(fields, tables, phase):
    fwd_left, inv_left, fwd_right, inv_right, twiddle = tables
    tw_real, tw_imag = twiddle[0], twiddle[1]
    value = jnp.concatenate([jnp.concatenate(pair, 0) for pair in fields], 1)
    value = apply_left(fwd_left[...], value)
    pieces = []
    for i in range(2):
        lanes = slice(i * 128, (i + 1) * 128)
        pieces.append(
            jnp.concatenate(
                times(value[:128, lanes], value[128:, lanes], tw_real, tw_imag), 1
            )
        )
    value = apply_right(jnp.concatenate(pieces, 0), fwd_right[...])
    ph_real, ph_imag = phase[0], phase[1]
    pieces = []
    for i in range(2):
        rows = slice(i * 128, (i + 1) * 128)
        pieces.append(
            jnp.concatenate(
                times(value[rows, :128], value[rows, 128:], ph_real, ph_imag), 1
            )
        )
    value = apply_right(jnp.concatenate(pieces, 0), inv_right[...])
    pieces = []
    for i in range(2):
        rows = slice(i * 128, (i + 1) * 128)
        pieces.append(
            jnp.concatenate(
                times(value[rows, :128], value[rows, 128:], tw_real, -tw_imag), 0
            )
        )
    value = apply_left(inv_left[...], jnp.concatenate(pieces, 1))
    return [
        (value[:128, i * 128 : (i + 1) * 128], value[128:, i * 128 : (i + 1) * 128])
        for i in range(2)
    ]


def target_of(chip, step):
    offset = (step * 37) % CHIPS
    x = (chip // 32 + offset // 32) % 4
    y = ((chip // 8) % 4 + (offset // 8) % 4) % 4
    z = (chip % 8 + offset % 8) % 8
    return x * 32 + y * 8 + z


def send_all(chip, core, source, landing, send_sem, recv_sem):
    def one(step, carry):
        goal = target_of(chip, step)
        for goal_core in range(2):
            own = jnp.logical_and(step == 0, core == goal_core)

            @pl.when(jnp.logical_not(own))
            def _():
                pltpu.make_async_remote_copy(
                    source(goal, goal_core),
                    landing,
                    send_sem,
                    recv_sem,
                    device_id=(goal, goal_core),
                    device_id_type=MESH,
                ).start()

            @pl.when(own)
            def _():
                pltpu.make_async_copy(
                    source(goal, goal_core), landing, recv_sem
                ).start()

        return carry

    lax.fori_loop(0, CHIPS, one, 0)


def drain(view, sem):
    pltpu.make_async_copy(view, view, sem).wait()


def middle_kernel(
    heights,
    wind_cols,
    wind_rows,
    screen,
    strip,
    y0, y1, y2, y3, y4,
    x0, x1, x2, x3, x4,
    out,
    work,
    field_out,
    field_in,
    screen_out,
    screen_in,
    back_out,
    back_in,
    phase_y,
    phase_a,
    phase_b,
    field_send,
    field_recv,
    screen_send,
    screen_recv,
    back_send,
    back_recv,
):
    chip = lax.axis_index("col")
    core = lax.axis_index("layer")
    device = chip * 2 + core
    tables_of_y = (y0, y1, y2, y3, y4)
    tables_of_x = (x0, x1, x2, x3, x4)

    barrier = pltpu.get_barrier_semaphore()

    def greet(step, carry):
        goal = target_of(chip, step)

        @pl.when(step > 0)
        def _():
            pl.semaphore_signal(
                barrier, inc=1, device_id=(goal, core), device_id_type=MESH
            )

        pl.semaphore_signal(
            barrier, inc=1, device_id=(goal, 1 - core), device_id_type=MESH
        )
        return carry

    lax.fori_loop(0, CHIPS, greet, 0)

    least = REACH - wind_cols[core]
    row = lax.broadcasted_iota(jnp.int32, (REACH, LANES), 0)
    fresh = jnp.logical_and(chip == CHIPS - 1, row >= least)

    def unmoved(tile):
        lanes = pl.ds(pl.multiple_of(tile * LANES, LANES), LANES)
        edge = jnp.where(fresh, strip[0, :, lanes], screen[0, pl.ds(REACH, REACH), lanes])
        return jnp.concatenate([screen[0, pl.ds(0, REACH), lanes], edge], 0)

    @pl.when(core == 0)
    def _():
        symbol_y(phase_y, heights[0], wind_rows[0] - wind_rows[1])

        def start(tile, carry):
            rows = pl.ds(pl.multiple_of(tile * SPAN, SPAN), SPAN)
            work[0, rows, :], work[1, rows, :] = cos_sin(unmoved(tile))
            return carry

        lax.fori_loop(0, 64, start, 0)
        along_y(work, work, SPAN, tables_of_y, phase_y)

        def turn(tile, carry):
            rows = pl.ds(pl.multiple_of(tile * LANES, LANES), LANES)
            for part in range(2):
                lower = work[part, pl.ds(pl.multiple_of(tile * SPAN, SPAN), SPAN), :]
                upper = work[part, pl.ds(pl.multiple_of((tile + 32) * SPAN, SPAN), SPAN), :]
                field_out[part, rows, :] = jnp.concatenate([lower, upper], 0).T
            return carry

        lax.fori_loop(0, 32, turn, 0)

    @pl.when(core == 1)
    def _():
        def turn(tile, carry):
            rows = pl.ds(pl.multiple_of(tile * LANES, LANES), LANES)
            both = jnp.concatenate([unmoved(tile), unmoved(tile + 32)], 0)
            screen_out[rows, :] = both.T
            return carry

        lax.fori_loop(0, 32, turn, 0)

    pl.semaphore_wait(barrier, DEVICES - 1)

    slot = pl.ds(pl.multiple_of(chip * 8, 8), 8)

    @pl.when(core == 0)
    def _():
        def source(goal, goal_core):
            rows = pl.ds(pl.multiple_of((goal * 2 + goal_core) * 8, 8), 8)
            return field_out.reshape(2, 2, 2048, LANES).at[:, :, rows, :]

        send_all(chip, core, source, field_in.at[:, :, slot, :], field_send, field_recv)

    @pl.when(core == 1)
    def _():
        def source(goal, goal_core):
            rows = pl.ds(pl.multiple_of((goal * 2 + goal_core) * 8, 8), 8)
            return screen_out.reshape(2, 2048, LANES).at[:, rows, :]

        send_all(chip, core, source, screen_in.at[:, slot, :], screen_send, screen_recv)

    symbol_x(phase_a, heights[0], wind_cols[0] - wind_cols[1])
    symbol_x(phase_b, heights[1], wind_cols[1])

    drain(screen_in, screen_recv)
    drain(field_in, field_recv)

    lane = lax.broadcasted_iota(jnp.int32, (CHIPS, LANES), 1)
    odd = (lane // 32) % 2 == 1

    def rows_of(step, carry):
        rows = pl.ds(step, CHIPS, stride=STEPS)
        fields = [(field_in[0, i, rows, :], field_in[1, i, rows, :]) for i in range(2)]
        fields = along_x(fields, tables_of_x, phase_a)
        fields = [
            times(*fields[i], *cos_sin(screen_in[i, rows, :])) for i in range(2)
        ]
        fields = along_x(fields, tables_of_x, phase_b)
        for part in range(2):
            even_rows, odd_rows = fields[0][part], fields[1][part]
            back_out[part, 0, rows, :] = jnp.where(
                odd, pltpu.roll(odd_rows, 32, 1), even_rows
            )
            back_out[part, 1, rows, :] = jnp.where(
                odd, odd_rows, pltpu.roll(even_rows, 96, 1)
            )
        return carry

    lax.fori_loop(0, STEPS, rows_of, 0)

    def back_source(goal, goal_core):
        rows = pl.ds(pl.multiple_of(goal * 8, 8), 8)
        return back_out.at[:, goal_core, rows, :]

    own = pl.ds(pl.multiple_of(device * 8, 8), 8)
    send_all(chip, core, back_source, back_in.at[:, own, :], back_send, back_recv)

    @pl.when(core == 0)
    def _():
        sent = field_out.reshape(2, 2, 2048, LANES).at[:, :, pl.ds(0, 2040), :]
        drain(sent, field_send)

    @pl.when(core == 1)
    def _():
        sent = screen_out.reshape(2, 2048, LANES).at[:, pl.ds(0, 2040), :]
        drain(sent, screen_send)

    drain(back_in, back_recv)
    drain(back_in.at[:, pl.ds(0, 2040), :], back_send)
    out[...] = back_in[...]


def last_kernel(heights, wind_rows, came, y0, y1, y2, y3, y4, out, work, phase_y):
    symbol_y(phase_y, heights[1], wind_rows[1])

    def turn(tile, carry):
        rows = pl.ds(pl.multiple_of(tile * LANES, LANES), LANES)
        for part in range(2):
            turned_tile = came[part, rows, :].T
            for quarter in range(4):
                goal = pl.multiple_of((quarter * 16 + tile) * 32, 32)
                work[part, pl.ds(goal, 32), :] = turned_tile[quarter * 32 : quarter * 32 + 32]
        return carry

    lax.fori_loop(0, 16, turn, 0)
    along_y(work, work, 32, (y0, y1, y2, y3, y4), phase_y)

    def finish(tile, carry):
        lanes = pl.ds(pl.multiple_of(tile * LANES, LANES), LANES)
        rows = pl.ds(pl.multiple_of(tile * 32, 32), 32)
        for part in range(2):
            out[part, :, lanes] = work[part, rows, :]
        return carry

    lax.fori_loop(0, 64, finish, 0)


def passed_along(value, axis, steps):
    count = lax.axis_size(axis)
    return lax.ppermute(
        value, axis, [(source, source + steps) for source in range(count - steps)]
    )


def on_device(screens, strips, wind_cols, wind_rows, heights):
    group = lax.axis_index("layer")
    edge = screens[:, SPAN - REACH :, :]
    came = passed_along(edge, "col", 1)
    came = jnp.where(lax.axis_index("col") == 0, strips, came)
    extended = jnp.concatenate([came, screens], axis=1)
    start = REACH - wind_cols[group]
    window = lax.dynamic_slice_in_dim(extended[0], start, SPAN, 0)
    next_screens = jnp.roll(window, wind_rows[group], axis=1)[None]

    of_y = [jnp.asarray(table) for table in tables_y()]
    of_x = [jnp.asarray(table) for table in tables_x()]
    smem = pl.BlockSpec(memory_space=pltpu.SMEM)
    vmem = pl.BlockSpec(memory_space=pltpu.VMEM)
    middle = pl.pallas_call(
        middle_kernel,
        out_shape=jax.ShapeDtypeStruct((2, 2048, LANES), F32),
        in_specs=[smem] * 3 + [vmem] * 12,
        out_specs=vmem,
        scratch_shapes=[
            pltpu.VMEM((2, 4096, LANES), F32),
            pltpu.VMEM((2, 4096, LANES), F32),
            pltpu.VMEM((2, 2, 1024, LANES), F32),
            pltpu.VMEM((4096, LANES), F32),
            pltpu.VMEM((2, 1024, LANES), F32),
            pltpu.VMEM((2, 2, 1024, LANES), F32),
            pltpu.VMEM((2, 2048, LANES), F32),
            pltpu.VMEM((2, 64, LANES), F32),
            pltpu.VMEM((2, 128, LANES), F32),
            pltpu.VMEM((2, 128, LANES), F32),
        ]
        + [pltpu.SemaphoreType.DMA] * 6,
        compiler_params=pltpu.CompilerParams(
            collective_id=0, has_side_effects=True, vmem_limit_bytes=48 << 20
        ),
        name="middle",
    )(heights, wind_cols, wind_rows, screens, strips, *of_y, *of_x)
    field = pl.pallas_call(
        last_kernel,
        out_shape=jax.ShapeDtypeStruct((2, 32, SIZE), F32),
        in_specs=[smem] * 2 + [vmem] * 6,
        out_specs=vmem,
        scratch_shapes=[
            pltpu.VMEM((2, 2048, LANES), F32),
            pltpu.VMEM((2, 64, LANES), F32),
        ],
        compiler_params=pltpu.CompilerParams(vmem_limit_bytes=32 << 20),
        name="last",
    )(heights, wind_rows, middle, *of_y)
    return (field, next_screens)


def solution(mesh):
    placed = (P("layer", "col", None), P("layer", None, None), P(), P(), P())
    return jax.shard_map(
        on_device,
        mesh=mesh,
        in_specs=placed,
        out_specs=(P(None, ("col", "layer"), None), P("layer", "col", None)),
        check_vma=False,
    )
```

time: 659 us -> 198 us (0.30)
  local copies, waits for them, and re-layouts: 246 us -> 9.97 us
  Pallas kernels: 0 us -> 175 us
  blocking collectives: 156 us -> 0 us
  waiting for transfers between devices: 116 us -> 0.01 us
  other arithmetic: 67.5 us -> 2.92 us
  matrix products: 32.5 us -> 0 us
  starting transfers between devices: 29.9 us -> 5.35 us
    pallas_call x0 -> x2, Pallas kernels: none -> 175 us  [the longest x1 161 us: on_device(): pl.pallas_call(middle_kernel, out_shape=jax.ShapeDtypeStruct((2, 2048, LA...]
    all_to_all x7 -> x0, blocking collectives: 156 us -> none  [the longest x1 59.3 us: propagate(): lax.all_to_all(field, 'col', split_axis=2, concat_axis=1, tiled=True)]
    unnamed x75 -> x30, local copies, waits for them, and re-layouts: 120 us -> 6.4 us
    all_to_all x2 -> x0, waiting for transfers between devices: 99.2 us -> none  [the longest x1 50.6 us: propagate(): lax.all_to_all(field, 'col', split_axis=1, concat_axis=2, tiled=True)]
    all_to_all x15 -> x0, local copies, waits for them, and re-layouts: 70.3 us -> none  [the longest x4 29.5 us: propagate(): lax.all_to_all(field, 'col', split_axis=1, concat_axis=2, tiled=True)]
    all_to_all x6 -> x0, other arithmetic: 45.4 us -> none  [the longest x2 16.2 us: regroup(): lax.all_to_all(field, 'layer', split_axis=2, concat_axis=1, tiled=True)]
    reshape x8 -> x0, local copies, waits for them, and re-layouts: 33.5 us -> none  [the longest x4 15.7 us: forward_first(): field.reshape(parts, fwd_first.shape[1], fwd_second.shape[1], width)]
    dot_general x16 -> x0, matrix products: 32.5 us -> none  [complex_sum(): return jnp.einsum(form, field, table, precision=lax.Precision.HIGHEST)]
  transfers between devices with their start and end apart: 3 -> 1, of which waited for: 3 -> 0; matrix products, arithmetic and copies ran while one was open for 1% -> 1% of each run, Pallas kernels for 0% -> 89%
where the time goes in v1:
time: 198 us; the launch traced here: 197 us
  Pallas kernels  175 us (88%)
  local copies, waits for them, and re-layouts  9.97 us (5%)
  starting transfers between devices  5.35 us (3%)
  between operations  4.07 us (2%)
  other arithmetic  2.92 us (1%)
    pallas_call x1, Pallas kernels, on_device(): pl.pallas_call(middle_kernel, out_shape=jax.ShapeDtypeStruct((2, 2048, LA...  161 us
    pallas_call x1, Pallas kernels, on_device(): pl.pallas_call(last_kernel, out_shape=jax.ShapeDtypeStruct((2, 32, SIZE),...  14.1 us
    unnamed x30, local copies, waits for them, and re-layouts  6.4 us
    ppermute x1, starting transfers between devices, passed_along(): lax.ppermute(value, axis, [(source, source + steps) for source in range(c...  5.35 us
  transfers between devices with their start and end apart: 1, of which 0 were waited for; matrix products, arithmetic and copies ran while one was open for 1% of the time, Pallas kernels for 89%

profile of v1, /device:TPU:1, one launch (start us, length us, event | category | flops | bytes accessed | tf_op | source)
XLA Modules:
  0.0 197.0 jit_solution(3353477425578060315)
XLA Ops:
  0.6 0.0 copy-start.9
  0.6 0.0 copy-start.1
  0.7 0.0 copy-start.2
  0.7 0.0 copy-start.3
  0.7 0.0 copy-start.4
  0.7 0.0 copy-start.12
  0.7 0.0 copy-start.13
  0.7 0.0 copy-start.11
  0.7 0.0 copy-start
  0.7 2.4 %slice.3 = f32[1,32,8192]{2,1,0:T(8,128)} slice(f32[1,64,8192]{2,1,0:T(8,128)} %screen.1), slice={[0:1], [32:64], [0:8192]} | slice | bytes 2097152 | tf_op jit(solution)/shard_map/slice | solution.py:494
  3.1 5.3 %collective-permute-start = (f32[1,32,8192]{2,1,0:T(8,128)}, f32[1,32,8192]{2,1,0:T(8,128)}, u32[]{:S(2)}, u32[]{:S(2)}) collective-permute-start(f32[1,32,8192]{2,1,0:T(8,128)} %slice.3), channel_id=1, source_target_pairs={{0,2},{2,4},{4,6},{6,8},{8,10},{10,12},{12,14},{14,16},{16,18},{18... | collective-permute-start | bytes 3145736 | tf_op jit(solution)/shard_map/ppermute | solution.py:487
  8.5 0.0 copy-done.12
  8.5 0.6 dynamic_slice.18
  11.0 0.0 copy-done.13
  11.0 0.6 dynamic_slice.15
  12.9 0.0 copy-done.9
  12.9 0.0 copy-done.1
  13.0 0.0 copy-done.2
  13.0 0.0 copy-done.3
  13.0 0.0 copy-start.5
  13.0 1.0 copy-done.5
  14.0 1.0 copy-done.6
  15.0 1.0 copy-done.7
  16.0 1.0 copy-done.8
  17.0 0.9 copy-done.10
  17.9 160.6 %middle.1.came = f32[2,2048,128]{2,1,0:T(8,128)S(1)} custom-call(s32[2]{0:T(128)S(1)} %copy-done.11, s32[2]{0:T(128)S(1)} %copy-done.13, s32[2]{0:T(128)S(1)} %copy-done.12, f32[1,64,8192]{2,1,0:T(8,128)} %screen.1, f32[1,32,8192]{2,1,0:T(8,128)S(1)} %copy-done, bf16[256,256]{1,0:T(8,128)(2,1)S(1)} %copy-done.4, bf16[256,256]{1,0:T(8,128)(2,1)S(1)} %copy-done.3, ...), custom_call_target="tpu_custom_call" | custom-call | tf_op jit(solution)/shard_map/middle/pallas_call | solution.py:506
  178.5 14.1 %last.1 = f32[2,32,8192]{2,1,0:T(8,128)} custom-call(s32[2]{0:T(128)S(1)} %copy-done.11, s32[2]{0:T(128)S(1)} %copy-done.12, f32[2,2048,128]{2,1,0:T(8,128)S(1)} %middle.1.came, bf16[256,256]{1,0:T(8,128)(2,1)S(1)} %copy-done.4, bf16[256,256]{1,0:T(8,128)(2,1)S(1)} %copy-done.3, bf16[768,256]{1,0:T(8,128)(2,1)S(1)} %copy-done.2, ...), custom_call_target="tpu_custom_call" | custom-call | tf_op jit(solution)/shard_map/last/pallas_call | solution.py:529
  192.6 0.0 collective-permute-done
  192.6 0.1 broadcast_select_fusion
  192.7 1.5 copy-done.14
  194.2 0.3 fusion.1
  194.5 2.5 %fusion.3 = f32[1,64,8192]{2,1,0:T(8,128)} fusion(s32[]{:T(128)S(6)} %select_n.33, f32[64,8192]{1,0:T(8,128)S(1)} %fusion.1), kind=kLoop, calls=%fused_computation.7 | loop fusion | flops 524288 | bytes 4194308 | tf_op jit(solution)/shard_map/broadcast_in_dim | solution.py:500
  (8 shorter events, 0.0 us)
Async XLA Ops:
  0.6 12.3 %copy-start.9 = (f32[2,64,128]{2,1,0:T(8,128)S(1)}, f32[2,64,128]{2,1,0:T(8,128)}, u32[]{:S(2)}) copy-start(f32[2,64,128]{2,1,0:T(8,128)} %constant.65.clone.y4) | copy-start | bytes 196612
  0.6 12.3 %copy-start.1 = (bf16[768,256]{1,0:T(8,128)(2,1)S(1)}, bf16[768,256]{1,0:T(8,128)(2,1)}, u32[]{:S(2)}) copy-start(bf16[768,256]{1,0:T(8,128)(2,1)} %constant.64.clone.y3) | copy-start | bytes 1179652
  0.7 12.3 %copy-start.2 = (bf16[768,256]{1,0:T(8,128)(2,1)S(1)}, bf16[768,256]{1,0:T(8,128)(2,1)}, u32[]{:S(2)}) copy-start(bf16[768,256]{1,0:T(8,128)(2,1)} %constant.63.clone.y2) | copy-start | bytes 1179652
  0.7 12.3 %copy-start.3 = (bf16[256,256]{1,0:T(8,128)(2,1)S(1)}, bf16[256,256]{1,0:T(8,128)(2,1)}, u32[]{:S(2)}) copy-start(bf16[256,256]{1,0:T(8,128)(2,1)} %constant.62.clone.y1) | copy-start | bytes 393220
  0.7 12.3 %copy-start.4 = (bf16[256,256]{1,0:T(8,128)(2,1)S(1)}, bf16[256,256]{1,0:T(8,128)(2,1)}, u32[]{:S(2)}) copy-start(bf16[256,256]{1,0:T(8,128)(2,1)} %constant.61.clone.y0) | copy-start | bytes 393220
  0.7 7.8 %copy-start.12 = (s32[2]{0:T(128)S(1)}, s32[2]{0:T(128)}, u32[]{:S(2)}) copy-start(s32[2]{0:T(128)} %wind_rows.3) | copy-start | bytes 28
  0.7 10.3 %copy-start.13 = (s32[2]{0:T(128)S(1)}, s32[2]{0:T(128)}, u32[]{:S(2)}) copy-start(s32[2]{0:T(128)} %wind_cols.1) | copy-start | bytes 28
  0.7 12.3 %copy-start.11 = (s32[2]{0:T(128)S(1)}, s32[2]{0:T(128)}, u32[]{:S(2)}) copy-start(s32[2]{0:T(128)} %heights.3) | copy-start | bytes 28
  0.7 12.3 %copy-start = (f32[1,32,8192]{2,1,0:T(8,128)S(1)}, f32[1,32,8192]{2,1,0:T(8,128)}, u32[]{:S(2)}) copy-start(f32[1,32,8192]{2,1,0:T(8,128)} %strip.1) | copy-start | bytes 3145732
  3.1 189.4 %collective-permute-start = (f32[1,32,8192]{2,1,0:T(8,128)}, f32[1,32,8192]{2,1,0:T(8,128)}, u32[]{:S(2)}, u32[]{:S(2)}) collective-permute-start(f32[1,32,8192]{2,1,0:T(8,128)} %slice.3), channel_id=1, source_target_pairs={{0,2},{2,4},{4,6},{6,8},{8,10},{10,12},{12,14},{14,16},{16,18},{18... | collective-permute-start | bytes 3145736 | tf_op jit(solution)/shard_map/ppermute | solution.py:487
  13.0 1.0 copy-start.5
  14.0 1.0 copy-start.6
  15.0 1.0 copy-start.7
  16.0 1.0 copy-start.8
  17.0 0.9 copy-start.10
  192.6 1.6 copy-start.14

commit v2 on v1

--- a/solution.py
+++ b/solution.py
@@ -168,7 +168,7 @@
 
 def along_y(src, dst, width, tables, phase):
     fwd_left, inv_left, fwd_right, inv_right, twiddle = tables
-    together = 4
+    together = 16
 
     def body(group, carry):
         first = group * together
@@ -222,7 +222,7 @@
     value = jnp.concatenate([jnp.concatenate(pair, 0) for pair in fields], 1)
     value = apply_left(fwd_left[...], value)
     pieces = []
-    for i in range(2):
+    for i in range(len(fields)):
         lanes = slice(i * 128, (i + 1) * 128)
         pieces.append(
             jnp.concatenate(
@@ -232,7 +232,7 @@
     value = apply_right(jnp.concatenate(pieces, 0), fwd_right[...])
     ph_real, ph_imag = phase[0], phase[1]
     pieces = []
-    for i in range(2):
+    for i in range(len(fields)):
         rows = slice(i * 128, (i + 1) * 128)
         pieces.append(
             jnp.concatenate(
@@ -241,7 +241,7 @@
         )
     value = apply_right(jnp.concatenate(pieces, 0), inv_right[...])
     pieces = []
-    for i in range(2):
+    for i in range(len(fields)):
         rows = slice(i * 128, (i + 1) * 128)
         pieces.append(
             jnp.concatenate(
@@ -251,7 +251,7 @@
     value = apply_left(inv_left[...], jnp.concatenate(pieces, 1))
     return [
         (value[:128, i * 128 : (i + 1) * 128], value[128:, i * 128 : (i + 1) * 128])
-        for i in range(2)
+        for i in range(len(fields))
     ]
 
 
@@ -295,37 +295,60 @@
     pltpu.make_async_copy(view, view, sem).wait()
 
 
+def tables_in(sources, places, sems, first):
+    copies = [
+        pltpu.make_async_copy(source, place, sems.at[first + i])
+        for i, (source, place) in enumerate(zip(sources, places))
+    ]
+    for copy in copies:
+        copy.start()
+    return copies
+
+
 def middle_kernel(
     heights,
     wind_cols,
     wind_rows,
-    screen,
-    strip,
-    y0, y1, y2, y3, y4,
-    x0, x1, x2, x3, x4,
-    out,
-    work,
-    field_out,
-    field_in,
-    screen_out,
-    screen_in,
-    back_out,
-    back_in,
-    phase_y,
-    phase_a,
-    phase_b,
-    field_send,
-    field_recv,
-    screen_send,
-    screen_recv,
-    back_send,
-    back_recv,
+    *refs,
 ):
+    screen_hbm, strip_hbm = refs[:2]
+    tables_hbm = refs[2:12]
+    back_hbm, came_hbm = refs[12:14]
+    screen, strip = refs[14:16]
+    tables = refs[16:26]
+    (
+        work,
+        field_out,
+        field_in,
+        screen_out,
+        screen_in,
+        back_out,
+        back_in,
+        came,
+        phase_y,
+        phase_a,
+        phase_b,
+        load_sems,
+        field_send,
+        field_recv,
+        screen_send,
+        screen_recv,
+        back_send,
+        back_recv,
+        halo_send,
+        halo_recv,
+    ) = refs[26:]
     chip = lax.axis_index("col")
     core = lax.axis_index("layer")
     device = chip * 2 + core
-    tables_of_y = (y0, y1, y2, y3, y4)
-    tables_of_x = (x0, x1, x2, x3, x4)
+    tables_of_y, tables_of_x = tables[:5], tables[5:]
+
+    loads = tables_in(
+        (screen_hbm.at[0], strip_hbm.at[0]) + tuple(tables_hbm),
+        (screen, strip) + tuple(tables),
+        load_sems,
+        0,
+    )
 
     barrier = pltpu.get_barrier_semaphore()
 
@@ -351,8 +374,11 @@
 
     def unmoved(tile):
         lanes = pl.ds(pl.multiple_of(tile * LANES, LANES), LANES)
-        edge = jnp.where(fresh, strip[0, :, lanes], screen[0, pl.ds(REACH, REACH), lanes])
-        return jnp.concatenate([screen[0, pl.ds(0, REACH), lanes], edge], 0)
+        edge = jnp.where(fresh, strip[:, lanes], screen[pl.ds(REACH, REACH), lanes])
+        return jnp.concatenate([screen[pl.ds(0, REACH), lanes], edge], 0)
+
+    for copy in loads:
+        copy.wait()
 
     @pl.when(core == 0)
     def _():
@@ -364,17 +390,6 @@
             return carry
 
         lax.fori_loop(0, 64, start, 0)
-        along_y(work, work, SPAN, tables_of_y, phase_y)
-
-        def turn(tile, carry):
-            rows = pl.ds(pl.multiple_of(tile * LANES, LANES), LANES)
-            for part in range(2):
-                lower = work[part, pl.ds(pl.multiple_of(tile * SPAN, SPAN), SPAN), :]
-                upper = work[part, pl.ds(pl.multiple_of((tile + 32) * SPAN, SPAN), SPAN), :]
-                field_out[part, rows, :] = jnp.concatenate([lower, upper], 0).T
-            return carry
-
-        lax.fori_loop(0, 32, turn, 0)
 
     @pl.when(core == 1)
     def _():
@@ -390,57 +405,102 @@
 
     slot = pl.ds(pl.multiple_of(chip * 8, 8), 8)
 
+    def pass_edge(tile, carry):
+        lanes = pl.ds(pl.multiple_of(tile * LANES, LANES), LANES)
+        pltpu.make_async_remote_copy(
+            screen.at[pl.ds(REACH, REACH), lanes],
+            came.at[:, lanes],
+            halo_send,
+            halo_recv,
+            device_id=((chip + 1) % CHIPS, core),
+            device_id_type=MESH,
+        ).start()
+        return carry
+
     @pl.when(core == 0)
     def _():
-        def source(goal, goal_core):
-            rows = pl.ds(pl.multiple_of((goal * 2 + goal_core) * 8, 8), 8)
-            return field_out.reshape(2, 2, 2048, LANES).at[:, :, rows, :]
-
-        send_all(chip, core, source, field_in.at[:, :, slot, :], field_send, field_recv)
+        lax.fori_loop(0, 64, pass_edge, 0)
+        along_y(work, work, SPAN, tables_of_y, phase_y)
+
+        def turn(tile, carry):
+            rows = pl.ds(pl.multiple_of(tile * LANES, LANES), LANES)
+            lower = pl.ds(pl.multiple_of(tile * SPAN, SPAN), SPAN)
+            upper = pl.ds(pl.multiple_of((tile + 32) * SPAN, SPAN), SPAN)
+            for part in range(2):
+                both = jnp.concatenate([work[part, lower, :], work[part, upper, :]], 0)
+                field_out[part, rows, :] = both.T
+            return carry
+
+        lax.fori_loop(0, 32, turn, 0)
+
+        def send(half, carry):
+            def source(goal, goal_core):
+                rows = pl.ds(pl.multiple_of((goal * 2 + goal_core) * 8, 8), 8)
+                return field_out.reshape(2, 2, 2048, LANES).at[:, half, rows, :]
+
+            landing = field_in.at[:, half, slot, :]
+            send_all(chip, core, source, landing, field_send, field_recv.at[half])
+            return carry
+
+        lax.fori_loop(0, 2, send, 0)
 
     @pl.when(core == 1)
     def _():
-        def source(goal, goal_core):
-            rows = pl.ds(pl.multiple_of((goal * 2 + goal_core) * 8, 8), 8)
-            return screen_out.reshape(2, 2048, LANES).at[:, rows, :]
-
-        send_all(chip, core, source, screen_in.at[:, slot, :], screen_send, screen_recv)
+        def send(half, carry):
+            def source(goal, goal_core):
+                rows = pl.ds(pl.multiple_of((goal * 2 + goal_core) * 8, 8), 8)
+                return screen_out.reshape(2, 2048, LANES).at[half, rows, :]
+
+            landing = screen_in.at[half, slot, :]
+            send_all(chip, core, source, landing, screen_send, screen_recv.at[half])
+            return carry
+
+        lax.fori_loop(0, 2, send, 0)
+        lax.fori_loop(0, 64, pass_edge, 0)
 
     symbol_x(phase_a, heights[0], wind_cols[0] - wind_cols[1])
     symbol_x(phase_b, heights[1], wind_cols[1])
 
-    drain(screen_in, screen_recv)
-    drain(field_in, field_recv)
-
     lane = lax.broadcasted_iota(jnp.int32, (CHIPS, LANES), 1)
     odd = (lane // 32) % 2 == 1
-
-    def rows_of(step, carry):
-        rows = pl.ds(step, CHIPS, stride=STEPS)
-        fields = [(field_in[0, i, rows, :], field_in[1, i, rows, :]) for i in range(2)]
-        fields = along_x(fields, tables_of_x, phase_a)
-        fields = [
-            times(*fields[i], *cos_sin(screen_in[i, rows, :])) for i in range(2)
-        ]
-        fields = along_x(fields, tables_of_x, phase_b)
-        for part in range(2):
-            even_rows, odd_rows = fields[0][part], fields[1][part]
-            back_out[part, 0, rows, :] = jnp.where(
-                odd, pltpu.roll(odd_rows, 32, 1), even_rows
-            )
-            back_out[part, 1, rows, :] = jnp.where(
-                odd, odd_rows, pltpu.roll(even_rows, 96, 1)
-            )
+    own = pl.ds(pl.multiple_of(device * 8, 8), 8)
+
+    def half_of(half, carry):
+        drain(screen_in.at[half], screen_recv.at[half])
+        drain(field_in.at[:, half], field_recv.at[half])
+
+        def rows_of(step, carry):
+            slabs = [pl.ds(step * 4 + i, CHIPS, stride=STEPS) for i in range(4)]
+            fields = [
+                (field_in[0, half, rows, :], field_in[1, half, rows, :])
+                for rows in slabs
+            ]
+            fields = along_x(fields, tables_of_x, phase_a)
+            fields = [
+                times(*field, *cos_sin(screen_in[half, rows, :]))
+                for field, rows in zip(fields, slabs)
+            ]
+            fields = along_x(fields, tables_of_x, phase_b)
+            for (real, imag), rows in zip(fields, slabs):
+                back_out[half, 0, rows, :] = jnp.where(odd, pltpu.roll(imag, 32, 1), real)
+                back_out[half, 1, rows, :] = jnp.where(odd, imag, pltpu.roll(real, 96, 1))
+            return carry
+
+        lax.fori_loop(0, 2, rows_of, 0)
+
+        def source(goal, goal_core):
+            rows = pl.ds(pl.multiple_of(goal * 8, 8), 8)
+            return back_out.at[half, goal_core, rows, :]
+
+        landing = back_in.at[half, own, :]
+        send_all(chip, core, source, landing, back_send, back_recv.at[half])
         return carry
 
-    lax.fori_loop(0, STEPS, rows_of, 0)
-
-    def back_source(goal, goal_core):
-        rows = pl.ds(pl.multiple_of(goal * 8, 8), 8)
-        return back_out.at[:, goal_core, rows, :]
-
-    own = pl.ds(pl.multiple_of(device * 8, 8), 8)
-    send_all(chip, core, back_source, back_in.at[:, own, :], back_send, back_recv)
+    lax.fori_loop(0, 2, half_of, 0)
+
+    drain(came, halo_recv)
+    keep = pltpu.make_async_copy(came, came_hbm, load_sems.at[0])
+    keep.start()
 
     @pl.when(core == 0)
     def _():
@@ -452,25 +512,62 @@
         sent = screen_out.reshape(2, 2048, LANES).at[:, pl.ds(0, 2040), :]
         drain(sent, screen_send)
 
-    drain(back_in, back_recv)
+    drain(came, halo_send)
+    stores = []
+    for half in range(2):
+        drain(back_in.at[half], back_recv.at[half])
+        copy = pltpu.make_async_copy(
+            back_in.at[half], back_hbm.at[half], load_sems.at[1 + half]
+        )
+        copy.start()
+        stores.append(copy)
     drain(back_in.at[:, pl.ds(0, 2040), :], back_send)
-    out[...] = back_in[...]
-
-
-def last_kernel(heights, wind_rows, came, y0, y1, y2, y3, y4, out, work, phase_y):
+    for copy in stores + [keep]:
+        copy.wait()
+
+
+def last_kernel(heights, wind_cols, wind_rows, *refs):
+    back_hbm, came_hbm, screen_hbm, strip_hbm = refs[:4]
+    tables_hbm = refs[4:9]
+    out_hbm, next_hbm = refs[9:11]
+    back, extended = refs[11:13]
+    tables = refs[13:18]
+    out, moved, work, phase_y, sems = refs[18:]
+    chip = lax.axis_index("col")
+    core = lax.axis_index("layer")
+
+    loads = tables_in((back_hbm,) + tuple(tables_hbm), (back,) + tuple(tables), sems, 0)
+    screen_copy = pltpu.make_async_copy(
+        screen_hbm.at[0], extended.at[pl.ds(REACH, SPAN)], sems.at[6]
+    )
+    screen_copy.start()
+    edge = extended.at[pl.ds(0, REACH)]
+
+    @pl.when(chip == 0)
+    def _():
+        pltpu.make_async_copy(strip_hbm.at[0], edge, sems.at[7]).start()
+
+    @pl.when(chip != 0)
+    def _():
+        pltpu.make_async_copy(came_hbm, edge, sems.at[7]).start()
+
     symbol_y(phase_y, heights[1], wind_rows[1])
+    for copy in loads:
+        copy.wait()
 
     def turn(tile, carry):
         rows = pl.ds(pl.multiple_of(tile * LANES, LANES), LANES)
-        for part in range(2):
-            turned_tile = came[part, rows, :].T
-            for quarter in range(4):
-                goal = pl.multiple_of((quarter * 16 + tile) * 32, 32)
-                work[part, pl.ds(goal, 32), :] = turned_tile[quarter * 32 : quarter * 32 + 32]
+        for half in range(2):
+            tile_turned = back[half, rows, :].T
+            for upper in range(2):
+                goal = pl.multiple_of((upper * 32 + half * 16 + tile) * 32, 32)
+                for part in range(2):
+                    first = (upper * 2 + part) * 32
+                    work[part, pl.ds(goal, 32), :] = tile_turned[first : first + 32]
         return carry
 
     lax.fori_loop(0, 16, turn, 0)
-    along_y(work, work, 32, (y0, y1, y2, y3, y4), phase_y)
+    along_y(work, work, 32, tables, phase_y)
 
     def finish(tile, carry):
         lanes = pl.ds(pl.multiple_of(tile * LANES, LANES), LANES)
@@ -480,35 +577,56 @@
         return carry
 
     lax.fori_loop(0, 64, finish, 0)
-
-
-def passed_along(value, axis, steps):
-    count = lax.axis_size(axis)
-    return lax.ppermute(
-        value, axis, [(source, source + steps) for source in range(count - steps)]
-    )
+    out_copy = pltpu.make_async_copy(out, out_hbm, sems.at[0])
+    out_copy.start()
+
+    screen_copy.wait()
+    pltpu.make_async_copy(came_hbm, edge, sems.at[7]).wait()
+    up = (SPAN + wind_cols[core]) % (SPAN + REACH)
+    shift = wind_rows[core] & (SIZE - 1)
+    tiles, within = shift // LANES, shift % LANES
+    lane = lax.broadcasted_iota(jnp.int32, (SPAN, LANES), 1)
+
+    def source(tile):
+        lanes = pl.ds(pl.multiple_of(((tile - tiles) & 63) * LANES, LANES), LANES)
+        block = pltpu.roll(extended[:, lanes], up, 0)[:SPAN]
+        return pltpu.roll(block, within, 1)
+
+    def move(tile, before):
+        here = source(tile)
+        lanes = pl.ds(pl.multiple_of(tile * LANES, LANES), LANES)
+        moved[0, :, lanes] = jnp.where(lane >= within, here, before)
+        return here
+
+    lax.fori_loop(0, 64, move, source(-1))
+    next_copy = pltpu.make_async_copy(moved, next_hbm, sems.at[1])
+    next_copy.start()
+    out_copy.wait()
+    next_copy.wait()
 
 
 def on_device(screens, strips, wind_cols, wind_rows, heights):
-    group = lax.axis_index("layer")
-    edge = screens[:, SPAN - REACH :, :]
-    came = passed_along(edge, "col", 1)
-    came = jnp.where(lax.axis_index("col") == 0, strips, came)
-    extended = jnp.concatenate([came, screens], axis=1)
-    start = REACH - wind_cols[group]
-    window = lax.dynamic_slice_in_dim(extended[0], start, SPAN, 0)
-    next_screens = jnp.roll(window, wind_rows[group], axis=1)[None]
-
     of_y = [jnp.asarray(table) for table in tables_y()]
     of_x = [jnp.asarray(table) for table in tables_x()]
     smem = pl.BlockSpec(memory_space=pltpu.SMEM)
-    vmem = pl.BlockSpec(memory_space=pltpu.VMEM)
-    middle = pl.pallas_call(
+    anywhere = pl.BlockSpec(memory_space=pl.ANY)
+    places_y = [pltpu.VMEM(table.shape, table.dtype) for table in of_y]
+    places_x = [pltpu.VMEM(table.shape, table.dtype) for table in of_x]
+    back, came = pl.pallas_call(
         middle_kernel,
-        out_shape=jax.ShapeDtypeStruct((2, 2048, LANES), F32),
-        in_specs=[smem] * 3 + [vmem] * 12,
-        out_specs=vmem,
+        out_shape=(
+            jax.ShapeDtypeStruct((2, 2048, LANES), F32),
+            jax.ShapeDtypeStruct((REACH, SIZE), F32),
+        ),
+        in_specs=[smem] * 3 + [anywhere] * 12,
+        out_specs=(anywhere, anywhere),
         scratch_shapes=[
+            pltpu.VMEM((SPAN, SIZE), F32),
+            pltpu.VMEM((REACH, SIZE), F32),
+        ]
+        + places_y
+        + places_x
+        + [
             pltpu.VMEM((2, 4096, LANES), F32),
             pltpu.VMEM((2, 4096, LANES), F32),
             pltpu.VMEM((2, 2, 1024, LANES), F32),
@@ -516,29 +634,48 @@
             pltpu.VMEM((2, 1024, LANES), F32),
             pltpu.VMEM((2, 2, 1024, LANES), F32),
             pltpu.VMEM((2, 2048, LANES), F32),
+            pltpu.VMEM((REACH, SIZE), F32),
             pltpu.VMEM((2, 64, LANES), F32),
             pltpu.VMEM((2, 128, LANES), F32),
             pltpu.VMEM((2, 128, LANES), F32),
-        ]
-        + [pltpu.SemaphoreType.DMA] * 6,
+            pltpu.SemaphoreType.DMA((12,)),
+            pltpu.SemaphoreType.DMA,
+            pltpu.SemaphoreType.DMA((2,)),
+            pltpu.SemaphoreType.DMA,
+            pltpu.SemaphoreType.DMA((2,)),
+            pltpu.SemaphoreType.DMA,
+            pltpu.SemaphoreType.DMA((2,)),
+            pltpu.SemaphoreType.DMA,
+            pltpu.SemaphoreType.DMA,
+        ],
         compiler_params=pltpu.CompilerParams(
-            collective_id=0, has_side_effects=True, vmem_limit_bytes=48 << 20
+            collective_id=0, has_side_effects=True, vmem_limit_bytes=60 << 20
         ),
         name="middle",
     )(heights, wind_cols, wind_rows, screens, strips, *of_y, *of_x)
-    field = pl.pallas_call(
+    return pl.pallas_call(
         last_kernel,
-        out_shape=jax.ShapeDtypeStruct((2, 32, SIZE), F32),
-        in_specs=[smem] * 2 + [vmem] * 6,
-        out_specs=vmem,
+        out_shape=(
+            jax.ShapeDtypeStruct((2, 32, SIZE), F32),
+            jax.ShapeDtypeStruct((1, SPAN, SIZE), F32),
+        ),
+        in_specs=[smem] * 3 + [anywhere] * 9,
+        out_specs=(anywhere, anywhere),
         scratch_shapes=[
             pltpu.VMEM((2, 2048, LANES), F32),
+            pltpu.VMEM((REACH + SPAN, SIZE), F32),
+        ]
+        + places_y
+        + [
+            pltpu.VMEM((2, 32, SIZE), F32),
+            pltpu.VMEM((1, SPAN, SIZE), F32),
+            pltpu.VMEM((2, 2048, LANES), F32),
             pltpu.VMEM((2, 64, LANES), F32),
+            pltpu.SemaphoreType.DMA((8,)),
         ],
-        compiler_params=pltpu.CompilerParams(vmem_limit_bytes=32 << 20),
+        compiler_params=pltpu.CompilerParams(vmem_limit_bytes=60 << 20),
         name="last",
-    )(heights, wind_rows, middle, *of_y)
-    return (field, next_screens)
+    )(heights, wind_cols, wind_rows, back, came, screens, strips, *of_y)
 
 
 def solution(mesh):

time: 198 us -> 179 us (0.904)
  local copies, waits for them, and re-layouts: 9.97 us -> 0 us
  starting transfers between devices: 5.35 us -> 0 us
  Pallas kernels: 175 us -> 179 us
  between operations: 4.07 us -> 0.64 us
  other arithmetic: 2.92 us -> 0 us
    unnamed x30 -> x0, local copies, waits for them, and re-layouts: 6.4 us -> none
    ppermute x1 -> x0, starting transfers between devices: 5.35 us -> none  [passed_along(): lax.ppermute(value, axis, [(source, source + steps) for source in range(c...]
    pallas_call x2, Pallas kernels: 175 us -> 179 us  [the longest x1 161 us: on_device(): pl.pallas_call(middle_kernel, out_shape=(jax.ShapeDtypeStruct((2, 2048, L...]
    broadcast_in_dim x1 -> x0, other arithmetic: 2.48 us -> none  [on_device(): next_screens = jnp.roll(window, wind_rows[group], axis=1)[None]]
    slice x1 -> x0, local copies, waits for them, and re-layouts: 2.4 us -> none  [on_device(): edge = screens[:, SPAN - REACH:, :]]
  transfers between devices with their start and end apart: 1 -> 0, of which waited for: 0 -> 0; matrix products, arithmetic and copies ran while one was open for 1% -> 0% of each run, Pallas kernels for 89% -> 0%
where the time goes in v2:
time: 179 us
  Pallas kernels  179 us (100%)
    pallas_call x1, Pallas kernels, on_device(): pl.pallas_call(middle_kernel, out_shape=(jax.ShapeDtypeStruct((2, 2048, L...  161 us
    pallas_call x1, Pallas kernels, on_device(): pl.pallas_call(last_kernel, out_shape=(jax.ShapeDtypeStruct((2, 32, SIZE)...  17.4 us

profile of v2, /device:TPU:1, one launch (start us, length us, event | category | flops | bytes accessed | tf_op | source)
XLA Modules:
  0.0 179.2 jit_solution(1615635144385404750)
XLA Ops:
  0.6 161.1 %middle.1 = (f32[2,2048,128]{2,1,0:T(8,128)}, f32[32,8192]{1,0:T(8,128)}) custom-call(s32[2]{0:T(128)} %heights.3, s32[2]{0:T(128)} %wind_cols.3, s32[2]{0:T(128)} %wind_rows.3, f32[1,64,8192]{2,1,0:T(8,128)} %refs_2_.2, f32[1,32,8192]{2,1,0:T(8,128)} %refs_3_.2, bf16[256,256]{1,0:T(8,128)(2,1)} %constant.20.clone.refs_2_.refs_4_, ...), custom_call_target="tpu_custom_call" | custom-call | tf_op jit(solution)/shard_map/middle/pallas_call | solution.py:615
  161.8 17.4 %last.1 = (f32[2,32,8192]{2,1,0:T(8,128)}, f32[1,64,8192]{2,1,0:T(8,128)}) custom-call(s32[2]{0:T(128)} %heights.3, s32[2]{0:T(128)} %wind_cols.3, s32[2]{0:T(128)} %wind_rows.3, f32[2,2048,128]{2,1,0:T(8,128)} %get-tuple-element.4.refs_0_, f32[32,8192]{1,0:T(8,128)} %get-tuple-element.5.refs_1_, f32[1,64,8192]{2,1,0:T(8,128)} %refs_2_.2, ...), custom_call_target="tpu_custom_call" | custom-call | tf_op jit(solution)/shard_map/last/pallas_call | solution.py:656

commit v3 on v2

--- a/solution.py
+++ b/solution.py
@@ -20,6 +20,8 @@
 CHIPS = 128
 DEVICES = 256
 STEPS = 8
+EARLY = 32
+ORDER = (0, 1, 2, 3, 4, 5, 6, 7)
 
 
 def cut(table):
@@ -255,30 +257,40 @@
     ]
 
 
-def target_of(chip, step):
-    offset = (step * 37) % CHIPS
-    x = (chip // 32 + offset // 32) % 4
-    y = ((chip // 8) % 4 + (offset // 8) % 4) % 4
-    z = (chip % 8 + offset % 8) % 8
-    return x * 32 + y * 8 + z
-
-
-def send_all(chip, core, source, landing, send_sem, recv_sem):
-    def one(step, carry):
-        goal = target_of(chip, step)
+def every_chip(chip, visit):
+    x, y, z = chip // 32, (chip // 8) % 4, chip % 8
+    along_z = [(z + step) % 8 for step in ORDER]
+
+    def plane(step, carry):
+        base = ((x + step // 4) % 4) * 32 + ((y + step % 4) % 4) * 8
+        for steps, place in zip(ORDER, along_z):
+            visit(base + place, step == 0 if steps == 0 else None)
+        return carry
+
+    lax.fori_loop(0, 16, plane, 0)
+
+
+def send_all(core, source, landing, send_sem, recv_sem):
+    def remote(goal, goal_core):
+        pltpu.make_async_remote_copy(
+            source(goal, goal_core),
+            landing,
+            send_sem,
+            recv_sem,
+            device_id=(goal, goal_core),
+            device_id_type=MESH,
+        ).start()
+
+    def visit(goal, own_chip):
         for goal_core in range(2):
-            own = jnp.logical_and(step == 0, core == goal_core)
+            if own_chip is None:
+                remote(goal, goal_core)
+                continue
+            own = jnp.logical_and(own_chip, core == goal_core)
 
             @pl.when(jnp.logical_not(own))
             def _():
-                pltpu.make_async_remote_copy(
-                    source(goal, goal_core),
-                    landing,
-                    send_sem,
-                    recv_sem,
-                    device_id=(goal, goal_core),
-                    device_id_type=MESH,
-                ).start()
+                remote(goal, goal_core)
 
             @pl.when(own)
             def _():
@@ -286,9 +298,7 @@
                     source(goal, goal_core), landing, recv_sem
                 ).start()
 
-        return carry
-
-    lax.fori_loop(0, CHIPS, one, 0)
+    return visit
 
 
 def drain(view, sem):
@@ -313,7 +323,7 @@
 ):
     screen_hbm, strip_hbm = refs[:2]
     tables_hbm = refs[2:12]
-    back_hbm, came_hbm = refs[12:14]
+    out_hbm, came_hbm = refs[12:14]
     screen, strip = refs[14:16]
     tables = refs[16:26]
     (
@@ -325,6 +335,7 @@
         back_out,
         back_in,
         came,
+        out,
         phase_y,
         phase_a,
         phase_b,
@@ -352,21 +363,19 @@
 
     barrier = pltpu.get_barrier_semaphore()
 
-    def greet(step, carry):
-        goal = target_of(chip, step)
-
-        @pl.when(step > 0)
-        def _():
+    def greet(goal, own_chip):
+        def signal(goal_core):
             pl.semaphore_signal(
-                barrier, inc=1, device_id=(goal, core), device_id_type=MESH
+                barrier, inc=1, device_id=(goal, goal_core), device_id_type=MESH
             )
 
-        pl.semaphore_signal(
-            barrier, inc=1, device_id=(goal, 1 - core), device_id_type=MESH
-        )
-        return carry
-
-    lax.fori_loop(0, CHIPS, greet, 0)
+        if own_chip is None:
+            signal(core)
+        else:
+            pl.when(jnp.logical_not(own_chip))(lambda: signal(core))
+        signal(1 - core)
+
+    every_chip(chip, greet)
 
     least = REACH - wind_cols[core]
     row = lax.broadcasted_iota(jnp.int32, (REACH, LANES), 0)
@@ -419,7 +428,7 @@
 
     @pl.when(core == 0)
     def _():
-        lax.fori_loop(0, 64, pass_edge, 0)
+        lax.fori_loop(0, EARLY, pass_edge, 0)
         along_y(work, work, SPAN, tables_of_y, phase_y)
 
         def turn(tile, carry):
@@ -439,7 +448,7 @@
                 return field_out.reshape(2, 2, 2048, LANES).at[:, half, rows, :]
 
             landing = field_in.at[:, half, slot, :]
-            send_all(chip, core, source, landing, field_send, field_recv.at[half])
+            every_chip(chip, send_all(core, source, landing, field_send, field_recv.at[half]))
             return carry
 
         lax.fori_loop(0, 2, send, 0)
@@ -452,11 +461,11 @@
                 return screen_out.reshape(2, 2048, LANES).at[half, rows, :]
 
             landing = screen_in.at[half, slot, :]
-            send_all(chip, core, source, landing, screen_send, screen_recv.at[half])
+            every_chip(chip, send_all(core, source, landing, screen_send, screen_recv.at[half]))
             return carry
 
         lax.fori_loop(0, 2, send, 0)
-        lax.fori_loop(0, 64, pass_edge, 0)
+        lax.fori_loop(0, EARLY, pass_edge, 0)
 
     symbol_x(phase_a, heights[0], wind_cols[0] - wind_cols[1])
     symbol_x(phase_b, heights[1], wind_cols[1])
@@ -493,14 +502,17 @@
             return back_out.at[half, goal_core, rows, :]
 
         landing = back_in.at[half, own, :]
-        send_all(chip, core, source, landing, back_send, back_recv.at[half])
+        every_chip(chip, send_all(core, source, landing, back_send, back_recv.at[half]))
         return carry
 
     lax.fori_loop(0, 2, half_of, 0)
 
-    drain(came, halo_recv)
-    keep = pltpu.make_async_copy(came, came_hbm, load_sems.at[0])
-    keep.start()
+    lax.fori_loop(EARLY, 64, pass_edge, 0)
+
+    symbol_y(phase_y, heights[1], wind_rows[1])
+
+    def lanes_of(tile):
+        return pl.ds(pl.multiple_of(tile * LANES, LANES), LANES)
 
     @pl.when(core == 0)
     def _():
@@ -512,94 +524,91 @@
         sent = screen_out.reshape(2, 2048, LANES).at[:, pl.ds(0, 2040), :]
         drain(sent, screen_send)
 
-    drain(came, halo_send)
-    stores = []
     for half in range(2):
         drain(back_in.at[half], back_recv.at[half])
-        copy = pltpu.make_async_copy(
-            back_in.at[half], back_hbm.at[half], load_sems.at[1 + half]
-        )
-        copy.start()
-        stores.append(copy)
-    drain(back_in.at[:, pl.ds(0, 2040), :], back_send)
-    for copy in stores + [keep]:
-        copy.wait()
-
-
-def last_kernel(heights, wind_cols, wind_rows, *refs):
-    back_hbm, came_hbm, screen_hbm, strip_hbm = refs[:4]
-    tables_hbm = refs[4:9]
-    out_hbm, next_hbm = refs[9:11]
-    back, extended = refs[11:13]
-    tables = refs[13:18]
-    out, moved, work, phase_y, sems = refs[18:]
-    chip = lax.axis_index("col")
-    core = lax.axis_index("layer")
-
-    loads = tables_in((back_hbm,) + tuple(tables_hbm), (back,) + tuple(tables), sems, 0)
-    screen_copy = pltpu.make_async_copy(
-        screen_hbm.at[0], extended.at[pl.ds(REACH, SPAN)], sems.at[6]
-    )
-    screen_copy.start()
-    edge = extended.at[pl.ds(0, REACH)]
-
-    @pl.when(chip == 0)
-    def _():
-        pltpu.make_async_copy(strip_hbm.at[0], edge, sems.at[7]).start()
-
-    @pl.when(chip != 0)
-    def _():
-        pltpu.make_async_copy(came_hbm, edge, sems.at[7]).start()
-
-    symbol_y(phase_y, heights[1], wind_rows[1])
-    for copy in loads:
-        copy.wait()
-
-    def turn(tile, carry):
-        rows = pl.ds(pl.multiple_of(tile * LANES, LANES), LANES)
-        for half in range(2):
-            tile_turned = back[half, rows, :].T
+
+        def turn_back(tile, carry):
+            rows = pl.ds(pl.multiple_of(tile * LANES, LANES), LANES)
+            tile_turned = back_in[half, rows, :].T
             for upper in range(2):
                 goal = pl.multiple_of((upper * 32 + half * 16 + tile) * 32, 32)
                 for part in range(2):
                     first = (upper * 2 + part) * 32
                     work[part, pl.ds(goal, 32), :] = tile_turned[first : first + 32]
-        return carry
-
-    lax.fori_loop(0, 16, turn, 0)
-    along_y(work, work, 32, tables, phase_y)
+            return carry
+
+        lax.fori_loop(0, 16, turn_back, 0)
+    along_y(work, work, 32, tables_of_y, phase_y)
 
     def finish(tile, carry):
-        lanes = pl.ds(pl.multiple_of(tile * LANES, LANES), LANES)
         rows = pl.ds(pl.multiple_of(tile * 32, 32), 32)
         for part in range(2):
-            out[part, :, lanes] = work[part, rows, :]
+            out[part, :, lanes_of(tile)] = work[part, rows, :]
         return carry
 
     lax.fori_loop(0, 64, finish, 0)
-    out_copy = pltpu.make_async_copy(out, out_hbm, sems.at[0])
-    out_copy.start()
-
+    result = pltpu.make_async_copy(out, out_hbm, load_sems.at[1])
+    result.start()
+
+    drain(came, halo_recv)
+
+    keep = pltpu.make_async_copy(came, came_hbm, load_sems.at[0])
+    keep.start()
+    drain(came, halo_send)
+    drain(back_in.at[:, pl.ds(0, 2040), :], back_send)
+    result.wait()
+    keep.wait()
+
+
+def last_kernel(wind_cols, wind_rows, *refs):
+    field_hbm, came_hbm, screen_hbm, strip_hbm, out_hbm, next_hbm = refs[:6]
+    extended, moved, field, sems = refs[6:]
+    chip = lax.axis_index("col")
+    core = lax.axis_index("layer")
+
+    edge = extended.at[pl.ds(0, REACH)]
+    screen_copy = pltpu.make_async_copy(
+        screen_hbm.at[0], extended.at[pl.ds(REACH, SPAN)], sems.at[0]
+    )
+    screen_copy.start()
+
+    @pl.when(chip == 0)
+    def _():
+        pltpu.make_async_copy(strip_hbm.at[0], edge, sems.at[1]).start()
+
+    @pl.when(chip != 0)
+    def _():
+        pltpu.make_async_copy(came_hbm, edge, sems.at[1]).start()
+
+    field_copy = pltpu.make_async_copy(field_hbm, field, sems.at[2])
+    field_copy.start()
     screen_copy.wait()
-    pltpu.make_async_copy(came_hbm, edge, sems.at[7]).wait()
+    pltpu.make_async_copy(came_hbm, edge, sems.at[1]).wait()
+
     up = (SPAN + wind_cols[core]) % (SPAN + REACH)
     shift = wind_rows[core] & (SIZE - 1)
     tiles, within = shift // LANES, shift % LANES
-    lane = lax.broadcasted_iota(jnp.int32, (SPAN, LANES), 1)
+    kept = lax.broadcasted_iota(jnp.int32, (SPAN, LANES), 1) >= within
 
     def source(tile):
         lanes = pl.ds(pl.multiple_of(((tile - tiles) & 63) * LANES, LANES), LANES)
         block = pltpu.roll(extended[:, lanes], up, 0)[:SPAN]
         return pltpu.roll(block, within, 1)
 
-    def move(tile, before):
-        here = source(tile)
-        lanes = pl.ds(pl.multiple_of(tile * LANES, LANES), LANES)
-        moved[0, :, lanes] = jnp.where(lane >= within, here, before)
-        return here
-
-    lax.fori_loop(0, 64, move, source(-1))
-    next_copy = pltpu.make_async_copy(moved, next_hbm, sems.at[1])
+    def move(group, before):
+        for i in range(8):
+            tile = group * 8 + i
+            here = source(tile)
+            lanes = pl.ds(pl.multiple_of(tile * LANES, LANES), LANES)
+            moved[0, :, lanes] = jnp.where(kept, here, before)
+            before = here
+        return before
+
+    field_copy.wait()
+    out_copy = pltpu.make_async_copy(field, out_hbm, sems.at[2])
+    out_copy.start()
+    lax.fori_loop(0, 8, move, source(-1))
+    next_copy = pltpu.make_async_copy(moved, next_hbm, sems.at[3])
     next_copy.start()
     out_copy.wait()
     next_copy.wait()
@@ -612,10 +621,10 @@
     anywhere = pl.BlockSpec(memory_space=pl.ANY)
     places_y = [pltpu.VMEM(table.shape, table.dtype) for table in of_y]
     places_x = [pltpu.VMEM(table.shape, table.dtype) for table in of_x]
-    back, came = pl.pallas_call(
+    field, came = pl.pallas_call(
         middle_kernel,
         out_shape=(
-            jax.ShapeDtypeStruct((2, 2048, LANES), F32),
+            jax.ShapeDtypeStruct((2, REACH, SIZE), F32),
             jax.ShapeDtypeStruct((REACH, SIZE), F32),
         ),
         in_specs=[smem] * 3 + [anywhere] * 12,
@@ -635,6 +644,7 @@
             pltpu.VMEM((2, 2, 1024, LANES), F32),
             pltpu.VMEM((2, 2048, LANES), F32),
             pltpu.VMEM((REACH, SIZE), F32),
+            pltpu.VMEM((2, REACH, SIZE), F32),
             pltpu.VMEM((2, 64, LANES), F32),
             pltpu.VMEM((2, 128, LANES), F32),
             pltpu.VMEM((2, 128, LANES), F32),
@@ -656,26 +666,20 @@
     return pl.pallas_call(
         last_kernel,
         out_shape=(
-            jax.ShapeDtypeStruct((2, 32, SIZE), F32),
+            jax.ShapeDtypeStruct((2, REACH, SIZE), F32),
             jax.ShapeDtypeStruct((1, SPAN, SIZE), F32),
         ),
-        in_specs=[smem] * 3 + [anywhere] * 9,
+        in_specs=[smem] * 2 + [anywhere] * 4,
         out_specs=(anywhere, anywhere),
         scratch_shapes=[
-            pltpu.VMEM((2, 2048, LANES), F32),
             pltpu.VMEM((REACH + SPAN, SIZE), F32),
-        ]
-        + places_y
-        + [
-            pltpu.VMEM((2, 32, SIZE), F32),
             pltpu.VMEM((1, SPAN, SIZE), F32),
-            pltpu.VMEM((2, 2048, LANES), F32),
-            pltpu.VMEM((2, 64, LANES), F32),
-            pltpu.SemaphoreType.DMA((8,)),
+            pltpu.VMEM((2, REACH, SIZE), F32),
+            pltpu.SemaphoreType.DMA((4,)),
         ],
         compiler_params=pltpu.CompilerParams(vmem_limit_bytes=60 << 20),
         name="last",
-    )(heights, wind_cols, wind_rows, back, came, screens, strips, *of_y)
+    )(wind_cols, wind_rows, field, came, screens, strips)
 
 
 def solution(mesh):

time: 179 us -> 161 us (0.90)
  Pallas kernels: 179 us -> 160 us
    pallas_call x2, Pallas kernels: 179 us -> 160 us  [the longest x1 155 us: on_device(): pl.pallas_call(middle_kernel, out_shape=(jax.ShapeDtypeStruct((2, REACH,...]
where the time goes in v3:
time: 161 us
  Pallas kernels  160 us (99%)
    pallas_call x1, Pallas kernels, on_device(): pl.pallas_call(middle_kernel, out_shape=(jax.ShapeDtypeStruct((2, REACH,...  155 us
    pallas_call x1, Pallas kernels, on_device(): pl.pallas_call(last_kernel, out_shape=(jax.ShapeDtypeStruct((2, REACH, SI...  5.85 us

profile of v3, /device:TPU:1, one launch (start us, length us, event | category | flops | bytes accessed | tf_op | source)
XLA Modules:
  0.0 161.0 jit_solution(13791143556099698833)
XLA Ops:
  0.6 154.5 %middle.1 = (f32[2,32,8192]{2,1,0:T(8,128)}, f32[32,8192]{1,0:T(8,128)}) custom-call(s32[2]{0:T(128)} %heights.1, s32[2]{0:T(128)} %wind_cols.3, s32[2]{0:T(128)} %wind_rows.3, f32[1,64,8192]{2,1,0:T(8,128)} %refs_2_.2, f32[1,32,8192]{2,1,0:T(8,128)} %refs_3_.2, bf16[256,256]{1,0:T(8,128)(2,1)} %constant.20.clone.refs_2_, ...), custom_call_target="tpu_custom_call" | custom-call | tf_op jit(solution)/shard_map/middle/pallas_call | solution.py:624
  155.2 5.9 %last.1 = (f32[2,32,8192]{2,1,0:T(8,128)}, f32[1,64,8192]{2,1,0:T(8,128)}) custom-call(s32[2]{0:T(128)} %wind_cols.3, s32[2]{0:T(128)} %wind_rows.3, f32[2,32,8192]{2,1,0:T(8,128)} %get-tuple-element.4.refs_0_, f32[32,8192]{1,0:T(8,128)} %get-tuple-element.5.refs_1_, f32[1,64,8192]{2,1,0:T(8,128)} %refs_2_.2, f32[1,32,8192]{2,1,0:T(8,128)} %refs_3_.2), custom_call_target="tpu_custom_call" | custom-call | tf_op jit(solution)/shard_map/last/pallas_call | solution.py:666

commit v4 on v3

--- a/solution.py
+++ b/solution.py
@@ -21,7 +21,7 @@
 DEVICES = 256
 STEPS = 8
 EARLY = 32
-ORDER = (0, 1, 2, 3, 4, 5, 6, 7)
+ORDER = (1, 7, 2, 6, 3, 5, 4, 0)
 
 
 def cut(table):

time: 161 us -> 161 us (level)
  no operation moved by 1% of the time
where the time goes in v4:
time: 161 us
  Pallas kernels  161 us (100%)
    pallas_call x1, Pallas kernels, on_device(): pl.pallas_call(middle_kernel, out_shape=(jax.ShapeDtypeStruct((2, REACH,...  155 us
    pallas_call x1, Pallas kernels, on_device(): pl.pallas_call(last_kernel, out_shape=(jax.ShapeDtypeStruct((2, REACH, SI...  5.85 us

profile of v4, /device:TPU:1, one launch (start us, length us, event | category | flops | bytes accessed | tf_op | source)
XLA Modules:
  0.0 161.2 jit_solution(5208984227611024141)
XLA Ops:
  0.6 154.7 %middle.1 = (f32[2,32,8192]{2,1,0:T(8,128)}, f32[32,8192]{1,0:T(8,128)}) custom-call(s32[2]{0:T(128)} %heights.1, s32[2]{0:T(128)} %wind_cols.3, s32[2]{0:T(128)} %wind_rows.3, f32[1,64,8192]{2,1,0:T(8,128)} %refs_2_.2, f32[1,32,8192]{2,1,0:T(8,128)} %refs_3_.2, bf16[256,256]{1,0:T(8,128)(2,1)} %constant.20.clone.refs_2_, ...), custom_call_target="tpu_custom_call" | custom-call | tf_op jit(solution)/shard_map/middle/pallas_call | solution.py:624
  155.3 5.9 %last.1 = (f32[2,32,8192]{2,1,0:T(8,128)}, f32[1,64,8192]{2,1,0:T(8,128)}) custom-call(s32[2]{0:T(128)} %wind_cols.3, s32[2]{0:T(128)} %wind_rows.3, f32[2,32,8192]{2,1,0:T(8,128)} %get-tuple-element.4.refs_0_, f32[32,8192]{1,0:T(8,128)} %get-tuple-element.5.refs_1_, f32[1,64,8192]{2,1,0:T(8,128)} %refs_2_.2, f32[1,32,8192]{2,1,0:T(8,128)} %refs_3_.2), custom_call_target="tpu_custom_call" | custom-call | tf_op jit(solution)/shard_map/last/pallas_call | solution.py:666
